TPU v7x, 32 devices: a whole 2x2x4 slice. The times are simulated.
32 devices in a mesh: tm: 8 (over y, x, core), space: 4 (over z).
Axes of the slice: x: 2, y: 2, z: 4, core: 2. Of those that a mesh axis runs over, the one named last changes fastest.
Arguments:
- eigvec: bfloat16 [8, 2, 3, 4096, 384], P('tm', None, None, 'space'), may hold values from -1.5 to 1.5
- momenta: int32 [2, 3], replicated, may hold values from -2 to 2
- peram: bfloat16 [8, 2, 384, 4, 384], P('tm', None, 'space'), may hold values from -0.0078125 to 0.0078125
Outputs:
- dressed: bfloat16 [8, 384, 4, 2, 384], P('tm', 'space')
All inputs are finite; a program needn't handle non-finite values.
Results may differ from a plain program's by a relative error of at most 0.0073.
Values may be sent and summed in bfloat16 or wider, within the bound.
A program may use at most 128 MiB of HBM per device.

v0:
```python
import math

import jax
import jax.numpy as jnp
from jax import lax
from jax.sharding import PartitionSpec as P

SPIN = 4
COLORS = 3
LAT = 32


def partner(value, axis, stride):
    mask = 2**stride
    pairs = [(source, source ^ mask) for source in range(lax.axis_size(axis))]
    return lax.ppermute(value, axis, pairs)


def phase_gram(vectors, momentum, coord_x, coord_y, coord_z):
    sites_dev = vectors.shape[2]
    nvec = vectors.shape[3]
    winding = jnp.mod(momentum[0] * coord_x + momentum[1] * coord_y + momentum[2] * coord_z, LAT)
    theta = winding.astype(jnp.float32) * (2.0 * math.pi / LAT)
    cosine = jnp.cos(theta)[None, :, None]
    sine = jnp.sin(theta)[None, :, None]
    real_part = vectors[0].astype(jnp.float32)
    imag_part = vectors[1].astype(jnp.float32)
    phased_re = (cosine * real_part + sine * imag_part).astype(jnp.bfloat16)
    phased_im = (cosine * imag_part - sine * real_part).astype(jnp.bfloat16)
    upper = jnp.concatenate([phased_re, phased_im], axis=-1)
    lower = jnp.concatenate([phased_im, -phased_re], axis=-1)
    right = jnp.stack([upper, lower]).reshape(2 * COLORS * sites_dev, 2 * nvec)
    left = vectors.reshape(2 * COLORS * sites_dev, nvec)
    return lax.dot_general(
        left, right, (((0,), (0,)), ((), ())), preferred_element_type=jnp.float32
    )


def complex_left(block_re, block_im):
    rows = block_re.shape[0]
    cols = block_re.shape[1]
    stacked = jnp.stack(
        [
            jnp.concatenate([block_re, -block_im], axis=1),
            jnp.concatenate([block_im, block_re], axis=1),
        ],
        axis=1,
    )
    return stacked.reshape(2 * rows, 2 * cols)


def local(eigvec, momenta, peram):
    vectors = eigvec[0]
    sites_dev = vectors.shape[2]
    nvec = vectors.shape[3]
    nrows = peram.shape[2]
    sites = lax.axis_index("space") * sites_dev + jnp.arange(sites_dev, dtype=jnp.int32)
    coord_x = sites % LAT
    coord_y = sites // LAT % LAT
    coord_z = sites // (LAT * LAT)
    sink_part = phase_gram(vectors, momenta[0], coord_x, coord_y, coord_z)
    source_part = phase_gram(vectors, momenta[1], coord_x, coord_y, coord_z)
    bit_count = lax.axis_size("tm").bit_length() - 1
    share = lax.psum_scatter(source_part, "space", scatter_dimension=0, tiled=True).astype(
        jnp.bfloat16
    )
    for bit in range(bit_count):
        share = partner(share, "tm", bit)
    source = lax.all_gather(share, "space", axis=0, tiled=True)
    tau = peram[0].reshape(2, nrows, SPIN * nvec)
    offset = lax.axis_index("space") * nrows
    sink = lax.psum(sink_part, "space").astype(jnp.bfloat16)
    block_re = lax.dynamic_slice_in_dim(sink[:, :nvec], offset, nrows, 0)
    block_im = lax.dynamic_slice_in_dim(sink[:, nvec:], offset, nrows, 0)
    piece = lax.all_gather(tau, "space", axis=1, tiled=True)
    count = piece.shape[1]
    flat = piece.reshape(2 * count, SPIN * nvec)
    mixed = jnp.dot(
        complex_left(block_re, block_im), flat, preferred_element_type=jnp.float32
    ).reshape(nrows, 2, SPIN * nvec)
    mixed = mixed.astype(jnp.bfloat16)
    mixed_re = mixed[:, 0].reshape(nrows * SPIN, nvec)
    mixed_im = mixed[:, 1].reshape(nrows * SPIN, nvec)
    source_re = source[:, :nvec]
    source_im = source[:, nvec:]
    right = jnp.concatenate([source, jnp.concatenate([-source_im, source_re], axis=1)], axis=0)
    dressed = jnp.dot(
        jnp.concatenate([mixed_re, mixed_im], axis=1), right, preferred_element_type=jnp.float32
    )
    return dressed.reshape(1, nrows, SPIN, 2, nvec).astype(jnp.bfloat16)


def solution(mesh):
    return jax.shard_map(
        local,
        mesh=mesh,
        in_specs=(P("tm", None, None, "space", None), P(), P("tm", None, "space", None, None)),
        out_specs=P("tm", "space", None, None, None),
        check_vma=False,
    )
```

profile of v0, /device:TPU:0, one launch (start us, length us, event | category | flops | bytes accessed | tf_op | source)
XLA Modules:
  0.0 195.3 jit_solution(1949508081727052371)
XLA Ops:
  6.5 0.0 reduce-scatter.4.cloned.1.call-start
  6.5 1.6 fusion.45
  8.1 1.9 fusion.32
  10.1 1.9 fusion.34
  12.0 0.0 copy-start
  12.0 5.0 %fusion.39 = (bf16[3,1024,384]{2,1,0:T(8,128)(2,1)S(1)}, bf16[3,1024,384]{2,1,0:T(8,128)(2,1)}, bf16[3,1024,384]{2,1,0:T(8,128)(2,1)S(1)}, bf16[3,1024,384]{2,1,0:T(8,128)(2,1)S(1)}) fusion(bf16[1,2,3,1024,384]{4,3,2,1,0:T(8,128)(2,1)} %param.3, f32[1024]{0:T(1024)S(1)} %get-tuple-element.33, f32[1024]{0:T(1024)S(1)} %get-tuple-element.34, ...), kind=kLoop, calls=%fused_computation.81 | loop fusion | flops 14155776 | bytes 14172160 | tf_op jit(solution)/shard_map/neg | solution.py:31
  17.0 0.0 copy-done
  17.1 2.7 %fusion.3 = (bf16[3,1024,384]{2,1,0:T(8,128)(2,1)}, bf16[3,1024,384]{2,1,0:T(8,128)(2,1)S(1)}) fusion(f32[1024]{0:T(1024)S(1)} %get-tuple-element.33, f32[1024]{0:T(1024)S(1)} %get-tuple-element.34, bf16[1,2,3,1024,384]{4,3,2,1,0:T(8,128)(2,1)S(1)} %copy-done, f32[1024]{0:T(1024)S(1)} %get-tuple-element.35, f32[1024]{0:T(1024)S(1)} %get-tuple-element.36), kind=kLoop, calls=%fused_computation.13 | loop fusion | flops 11796480 | bytes 9453568 | tf_op jit(solution)/shard_map/convert_element_type | solution.py:29
  19.8 3.9 %maximum_bitcast_fusion.2 = (bf16[1,3,1024,768]{3,2,1,0:T(8,128)(2,1)}, bf16[1,3,1024,768]{3,2,1,0:T(8,128)(2,1)}) fusion(bf16[3,1024,384]{2,1,0:T(8,128)(2,1)S(1)} %get-tuple-element.12, bf16[3,1024,384]{2,1,0:T(8,128)(2,1)S(1)} %get-tuple-element.14, bf16[3,1024,384]{2,1,0:T(8,128)(2,1)S(1)} %get-tuple-element.13), kind=kLoop, calls=%fused_computation.20 | loop fusion | flops 18874368 | bytes 16515072 | tf_op jit(solution)/shard_map/stack | solution.py:32
  23.7 8.3 %pad_maximum_fusion.1 = bf16[2,3,1024,768]{3,2,1,0:T(8,128)(2,1)} fusion(bf16[1,3,1024,768]{3,2,1,0:T(8,128)(2,1)} %get-tuple-element.18, bf16[1,3,1024,768]{3,2,1,0:T(8,128)(2,1)} %get-tuple-element.17), kind=kLoop, calls=%fused_computation.1 | loop fusion | flops 4718592 | bytes 18874368 | tf_op jit(solution)/shard_map/stack | solution.py:32
  32.0 9.0 %convolution_bitcast_fusion = f32[384,768]{0,1:T(8,128)S(1)} fusion(bf16[6144,768]{1,0:T(8,128)(2,1)} %bitcast.56, bf16[6144,384]{1,0:T(8,128)(2,1)} %bitcast.54), kind=kOutput, calls=%fused_computation.23 | convolution fusion | flops 3623878656 | bytes 15335424 | tf_op jit(solution)/shard_map/dot_general | solution.py:34
  41.0 1.4 copy.8
  42.4 0.0 reduce-scatter.4.cloned.1.call-update
  42.4 0.0 all-gather.2.cloned.1.call-start
  42.4 2.2 %reshape_squeeze.14 = bf16[2,96,1536]{2,1,0:T(8,128)(2,1)} reshape(bf16[1,2,96,4,384]{4,3,2,1,0:T(4,128)(2,1)} %param.5) | data formatting | bytes 1179648 | tf_op jit(solution)/shard_map/reshape;squeeze | solution.py:70
  44.7 0.0 all-gather.2.cloned.1.call-update
  44.7 7.6 %maximum_bitcast_fusion = (bf16[1,3,1024,768]{3,2,1,0:T(8,128)(2,1)}, bf16[1,3,1024,768]{3,2,1,0:T(8,128)(2,1)}) fusion(bf16[3,1024,384]{2,1,0:T(8,128)(2,1)} %get-tuple-element.11, bf16[3,1024,384]{2,1,0:T(8,128)(2,1)} %get-tuple-element.8, bf16[3,1024,384]{2,1,0:T(8,128)(2,1)S(1)} %get-tuple-element.7), kind=kLoop, calls=%fused_computation.18 | loop fusion | flops 18874368 | bytes 16515072 | tf_op jit(solution)/shard_map/stack | solution.py:32
  52.4 8.3 %pad_maximum_fusion = bf16[2,3,1024,768]{3,2,1,0:T(8,128)(2,1)} fusion(bf16[1,3,1024,768]{3,2,1,0:T(8,128)(2,1)} %get-tuple-element.16, bf16[1,3,1024,768]{3,2,1,0:T(8,128)(2,1)} %get-tuple-element.15), kind=kLoop, calls=%fused_computation | loop fusion | flops 4718592 | bytes 18874368 | tf_op jit(solution)/shard_map/stack | solution.py:32
  60.7 9.1 %convolution_bitcast_fusion.1 = f32[384,768]{0,1:T(8,128)S(1)} fusion(bf16[6144,768]{1,0:T(8,128)(2,1)} %bitcast.57, bf16[6144,384]{1,0:T(8,128)(2,1)} %bitcast.55), kind=kOutput, calls=%fused_computation.24 | convolution fusion | flops 3623878656 | bytes 15335424 | tf_op jit(solution)/shard_map/dot_general | solution.py:34
  69.7 4.7 %reduce-scatter.4.cloned.1.call-done = f32[96,768]{1,0:T(8,128)} async-done(((f32[384,768]{1,0:T(8,128)}), f32[96,768]{1,0:T(8,128)}) %reduce-scatter.4.cloned.1.call-update) | async-done | bytes 294928
  74.4 1.1 copy.9
  75.5 0.1 collective-permute-start
  75.6 80.8 %all-reduce.1 = bf16[384,768]{0,1:T(8,128)(2,1)S(1)} all-reduce(f32[384,768]{0,1:T(8,128)S(1)} %convolution_bitcast_fusion.1), channel_id=1, replica_groups=mesh['tm'=8,'space'=4] {'space'}, use_global_device_ids=true, to_apply=%region_0.1 | all-reduce | flops 294912 | bytes 1769472 | tf_op jit(solution)/shard_map/psum | solution.py:72
  156.4 0.0 collective-permute-done
  156.4 1.3 collective-permute-start.1
  157.7 0.1 fusion.44
  157.8 0.1 fusion.38
  157.9 4.3 %collective-permute-done.1 = bf16[96,768]{0,1:T(8,128)(2,1)S(1)} collective-permute-done((bf16[96,768]{0,1:T(8,128)(2,1)S(1)}, bf16[96,768]{0,1:T(8,128)(2,1)S(1)}, u32[]{:S(2)}, u32[]{:S(2)}) %collective-permute-start.1) | collective-permute-done | bytes 147488 | tf_op jit(solution)/shard_map/ppermute | solution.py:16
  162.1 1.2 collective-permute-start.2
  163.3 0.1 constant_dynamic-slice_fusion.1
  163.5 0.1 maximum_bitcast_fusion.4
  163.5 4.3 %collective-permute-done.2 = bf16[96,768]{0,1:T(8,128)(2,1)S(1)} collective-permute-done((bf16[96,768]{0,1:T(8,128)(2,1)S(1)}, bf16[96,768]{0,1:T(8,128)(2,1)S(1)}, u32[]{:S(2)}, u32[]{:S(2)}) %collective-permute-start.2) | collective-permute-done | bytes 147488 | tf_op jit(solution)/shard_map/ppermute | solution.py:16
  167.8 0.1 copy.6
  167.9 16.1 %all_gather.7 = bf16[384,768]{1,0:T(8,128)(2,1)S(1)} all-gather(bf16[96,768]{1,0:T(8,128)(2,1)S(1)} %copy.6), channel_id=1, replica_groups=mesh['tm'=8,'space'=4] {'space'}, dimensions={0}, use_global_device_ids=true | all-gather | bytes 737280 | tf_op jit(solution)/shard_map/all_gather | solution.py:69
  184.0 0.1 slice_negate_fusion
  184.1 0.0 all-gather.2.cloned.1.call-done
  184.1 2.3 %convolution_convert_fusion = bf16[96,2,1536]{2,0,1:T(8,128)(2,1)S(1)} fusion(bf16[768,1536,1]{1,0,2:T(8,128)(2,1)} %bitcast.58, bf16[96,1,768]{0,2,1:T(8,128)(2,1)S(1)} %get-tuple-element.26, bf16[96,1,768]{0,2,1:T(8,128)(2,1)S(1)} %get-tuple-element.25), kind=kOutput, calls=%fused_computation.22 | convolution fusion | flops 453427200 | bytes 3244032 | tf_op jit(solution)/shard_map/dot_general | solution.py:78
  186.5 0.2 reshape_squeeze.15
  186.7 0.2 reshape_squeeze.16
  186.9 0.6 convolution_convert_fusion.1
  187.5 0.9 convert_element_type.83
  (1 shorter events, 0.0 us)
Async XLA Ops:
  6.5 67.9 %reduce-scatter.4.cloned.1.call-start = ((), (), s32[]{:S(2)}) async-start(), calls=%async_computation.2 | async-start | bytes 1474560
  12.0 5.1 %copy-start = (bf16[1,2,3,1024,384]{4,3,2,1,0:T(8,128)(2,1)S(1)}, bf16[1,2,3,1024,384]{4,3,2,1,0:T(8,128)(2,1)}, u32[]{:S(2)}) copy-start(bf16[1,2,3,1024,384]{4,3,2,1,0:T(8,128)(2,1)} %param.3) | copy-start | bytes 14155780
  42.4 141.7 %all-gather.2.cloned.1.call-start = ((), (), s32[]{:S(2)}) async-start(), calls=%async_computation.1 | async-start | bytes 2949120 | tf_op jit(solution)/shard_map/all_gather | solution.py:75
  75.5 80.9 %collective-permute-start = (bf16[96,768]{0,1:T(8,128)(2,1)S(1)}, bf16[96,768]{0,1:T(8,128)(2,1)S(1)}, u32[]{:S(2)}, u32[]{:S(2)}) collective-permute-start(bf16[96,768]{0,1:T(8,128)(2,1)S(1)} %copy.9), channel_id=1, source_target_pairs={{0,4},{4,0},{8,12},{12,8},{16,20},{20,16},{24,28},{28,24},{1,5},{5... | collective-permute-start | bytes 442376 | tf_op jit(solution)/shard_map/ppermute | solution.py:16
  156.4 5.7 %collective-permute-start.1 = (bf16[96,768]{0,1:T(8,128)(2,1)S(1)}, bf16[96,768]{0,1:T(8,128)(2,1)S(1)}, u32[]{:S(2)}, u32[]{:S(2)}) collective-permute-start(bf16[96,768]{0,1:T(8,128)(2,1)S(1)} %collective-permute-done), channel_id=1, source_target_pairs={{0,8},{4,12},{8,0},{12,4},{16,24},{20,28},{24,16},{28,20},{1,9},{5... | collective-permute-start | bytes 442376 | tf_op jit(solution)/shard_map/ppermute | solution.py:16
  162.1 5.7 %collective-permute-start.2 = (bf16[96,768]{0,1:T(8,128)(2,1)S(1)}, bf16[96,768]{0,1:T(8,128)(2,1)S(1)}, u32[]{:S(2)}, u32[]{:S(2)}) collective-permute-start(bf16[96,768]{0,1:T(8,128)(2,1)S(1)} %collective-permute-done.1), channel_id=1, source_target_pairs={{0,16},{4,20},{8,24},{12,28},{16,0},{20,4},{24,8},{28,12},{1,17},{... | collective-permute-start | bytes 442376 | tf_op jit(solution)/shard_map/ppermute | solution.py:16
Sparse Core Ops, SparseCore 0:
  42.5 31.8 reduce-scatter.3
  76.0 80.5 all-gather.1
where the time goes:
time: 196 us; the launch traced here: 195 us
  blocking collectives  96.9 us (49%)
  other arithmetic  40 us (20%)
  matrix products  21.1 us (11%)
  between operations  13.5 us (7%)
  waiting for transfers between devices  13.3 us (7%)
  local copies, waits for them, and re-layouts  7.96 us (4%)
  starting transfers between devices  2.6 us (1%)
    psum x1, blocking collectives, local(): sink = lax.psum(sink_part, 'space').astype(jnp.bfloat16)  80.8 us
    another operation x4, other arithmetic, phase_gram(): right = jnp.stack([upper, lower]).reshape(2 * COLORS * sites_dev, 2 * nvec)  28.1 us
    dot_general x2, matrix products, phase_gram(): lax.dot_general(left, right, (((0,), (0,)), ((), ())), preferred_element_...  18.1 us
    all_gather x1, blocking collectives, local(): source = lax.all_gather(share, 'space', axis=0, tiled=True)  16.1 us
    ppermute x3, waiting for transfers between devices, partner(): return lax.ppermute(value, axis, pairs)  8.56 us
    neg x1, other arithmetic, phase_gram(): lower = jnp.concatenate([phased_im, -phased_re], axis=-1)  5.04 us
    unnamed x3, waiting for transfers between devices  4.71 us
  transfers between devices with their start and end apart: 5, of which 3 were waited for; matrix products, arithmetic and copies ran while one was open for 15% of the time, Pallas kernels for 0%

commit v1 on v0

v1 whole, which is shorter than its diff:
```python
import functools
import math

import jax
import jax.numpy as jnp
from jax import lax
from jax.experimental import pallas as pl
from jax.experimental.pallas import tpu as pltpu
from jax.sharding import PartitionSpec as P

SPIN = 4
COLORS = 3
LAT = 32


def phase_tables(momenta_ref, k, first_site, count):
    sites = first_site + lax.broadcasted_iota(jnp.int32, (count, 128), 0)
    x = sites & (LAT - 1)
    y = (sites >> 5) & (LAT - 1)
    z = sites >> 10
    winding = (momenta_ref[k, 0] * x + momenta_ref[k, 1] * y + momenta_ref[k, 2] * z) & (LAT - 1)
    quadrant = (winding + 4) >> 3
    rest = (winding - (quadrant << 3)).astype(jnp.float32) * (2.0 * math.pi / LAT)
    sq = rest * rest
    sin_r = rest * (
        1.0 + sq * (-1.0 / 6 + sq * (1.0 / 120 + sq * (-1.0 / 5040 + sq * (1.0 / 362880))))
    )
    cos_r = 1.0 + sq * (
        -0.5 + sq * (1.0 / 24 + sq * (-1.0 / 720 + sq * (1.0 / 40320 + sq * (-1.0 / 3628800))))
    )
    odd = (quadrant & 1) == 1
    cos_q = jnp.where(odd, sin_r, cos_r)
    sin_q = jnp.where(odd, cos_r, sin_r)
    cos_t = jnp.where(((quadrant + 1) & 2) == 2, -cos_q, cos_q)
    sin_t = jnp.where((quadrant & 2) == 2, -sin_q, sin_q)
    return cos_t, sin_t


def gram_kernel(k, momenta_ref, vec_ref, out_ref, cos_ref, sin_ref, right_ref, acc_ref):
    step = pl.program_id(0)
    sites = vec_ref.shape[2]
    nvec = vec_ref.shape[3]

    @pl.when(step == 0)
    def _():
        first = lax.axis_index("space") * sites
        cos_t, sin_t = phase_tables(momenta_ref, k, first, sites)
        cos_ref[...] = cos_t
        sin_ref[...] = sin_t

    cosine = cos_ref[...]
    sine = sin_ref[...]
    for lane in range(0, nvec, 128):
        real = vec_ref[0, 0, :, lane : lane + 128].astype(jnp.float32)
        imag = vec_ref[1, 0, :, lane : lane + 128].astype(jnp.float32)
        ph_re = (cosine * real + sine * imag).astype(jnp.bfloat16)
        ph_im = (cosine * imag - sine * real).astype(jnp.bfloat16)
        right_ref[:sites, lane : lane + 128] = ph_re
        right_ref[:sites, nvec + lane : nvec + lane + 128] = ph_im
        right_ref[sites:, lane : lane + 128] = ph_im
        right_ref[sites:, nvec + lane : nvec + lane + 128] = -ph_re
    left = vec_ref[...].reshape(2 * sites, nvec)
    part = lax.dot_general(
        left, right_ref[...], (((0,), (0,)), ((), ())), preferred_element_type=jnp.float32
    )

    @pl.when(step == 0)
    def _():
        acc_ref[...] = part

    @pl.when(step > 0)
    def _():
        acc_ref[...] += part

    @pl.when(step == COLORS - 1)
    def _():
        out_ref[...] = acc_ref[...].astype(out_ref.dtype)


def gram(vectors, momenta, k, dtype):
    sites = vectors.shape[2]
    nvec = vectors.shape[3]
    return pl.pallas_call(
        functools.partial(gram_kernel, k),
        grid=(COLORS,),
        out_shape=jax.ShapeDtypeStruct((nvec, 2 * nvec), dtype),
        in_specs=[
            pl.BlockSpec(memory_space=pltpu.SMEM),
            pl.BlockSpec((2, 1, sites, nvec), lambda c: (0, c, 0, 0)),
        ],
        out_specs=pl.BlockSpec((nvec, 2 * nvec), lambda c: (0, 0)),
        scratch_shapes=[
            pltpu.VMEM((sites, 128), jnp.float32),
            pltpu.VMEM((sites, 128), jnp.float32),
            pltpu.VMEM((2 * sites, 2 * nvec), jnp.bfloat16),
            pltpu.VMEM((nvec, 2 * nvec), jnp.float32),
        ],
        compiler_params=pltpu.CompilerParams(vmem_limit_bytes=40 * 1024 * 1024),
        cost_estimate=pl.CostEstimate(
            flops=8 * COLORS * sites * nvec * nvec,
            bytes_accessed=4 * COLORS * sites * nvec,
            transcendentals=0,
        ),
    )(momenta, vectors)


def complex_left(block_re, block_im):
    rows = block_re.shape[0]
    cols = block_re.shape[1]
    stacked = jnp.stack(
        [
            jnp.concatenate([block_re, -block_im], axis=1),
            jnp.concatenate([block_im, block_re], axis=1),
        ],
        axis=1,
    )
    return stacked.reshape(2 * rows, 2 * cols)


def local(eigvec, momenta, peram):
    vectors = eigvec[0]
    nvec = vectors.shape[3]
    nrows = peram.shape[2]
    tau = peram[0].reshape(2, nrows, SPIN * nvec)
    source_part = gram(vectors, momenta, 1, jnp.float32)
    share = lax.psum_scatter(source_part, "space", scatter_dimension=0, tiled=True).astype(
        jnp.bfloat16
    )
    sink_part = gram(vectors, momenta, 0, jnp.float32)
    times = lax.axis_size("tm")
    share = lax.ppermute(share, "tm", [(i, times - 1 - i) for i in range(times)])
    source = lax.all_gather(share, "space", axis=0, tiled=True)
    block = lax.psum_scatter(sink_part, "space", scatter_dimension=0, tiled=True).astype(
        jnp.bfloat16
    )
    piece = lax.all_gather(tau, "space", axis=1, tiled=True)
    count = piece.shape[1]
    flat = piece.reshape(2 * count, SPIN * nvec)
    mixed = jnp.dot(
        complex_left(block[:, :nvec], block[:, nvec:]), flat, preferred_element_type=jnp.float32
    ).reshape(nrows, 2, SPIN * nvec)
    mixed = mixed.astype(jnp.bfloat16)
    mixed_re = mixed[:, 0].reshape(nrows * SPIN, nvec)
    mixed_im = mixed[:, 1].reshape(nrows * SPIN, nvec)
    source_re = source[:, :nvec]
    source_im = source[:, nvec:]
    right = jnp.concatenate([source, jnp.concatenate([-source_im, source_re], axis=1)], axis=0)
    dressed = jnp.dot(
        jnp.concatenate([mixed_re, mixed_im], axis=1), right, preferred_element_type=jnp.float32
    )
    return dressed.reshape(1, nrows, SPIN, 2, nvec).astype(jnp.bfloat16)


def solution(mesh):
    return jax.shard_map(
        local,
        mesh=mesh,
        in_specs=(P("tm", None, None, "space", None), P(), P("tm", None, "space", None, None)),
        out_specs=P("tm", "space", None, None, None),
        check_vma=False,
    )
```

time: 196 us -> 145 us (0.74)
  blocking collectives: 96.9 us -> 20.1 us
  waiting for transfers between devices: 13.3 us -> 78.6 us
  other arithmetic: 40 us -> 2.06 us
  matrix products: 21.1 us -> 2.92 us
  Pallas kernels: 0 us -> 16.5 us
    psum x1 -> x0, blocking collectives: 80.8 us -> none  [local(): sink = lax.psum(sink_part, 'space').astype(jnp.bfloat16)]
    reduce_scatter x0 -> x2, waiting for transfers between devices: none -> 46.2 us  [the longest x1 27.5 us: local(): lax.psum_scatter(sink_part, 'space', scatter_dimension=0, tiled=True)]
    all_gather x1, waiting for transfers between devices: 0.02 us -> 32.3 us  [local(): piece = lax.all_gather(tau, 'space', axis=1, tiled=True)]
    another operation x4 -> x0, other arithmetic: 28.1 us -> none  [phase_gram(): right = jnp.stack([upper, lower]).reshape(2 * COLORS * sites_dev, 2 * nvec)]
    dot_general x3 -> x1, matrix products: 20.4 us -> 2.29 us  [local(): jnp.dot(complex_left(block[:, :nvec], block[:, nvec:]), flat, preferred_e...]
    pallas_call x0 -> x2, Pallas kernels: none -> 16.5 us  [gram(): pl.pallas_call(functools.partial(gram_kernel, k), grid=(COLORS,), out_sha...]
    ppermute x3 -> x1, waiting for transfers between devices: 8.56 us -> 0.01 us  [local(): lax.ppermute(share, 'tm', [(i, times - 1 - i) for i in range(times)])]
    neg x1 -> x0, other arithmetic: 5.04 us -> none  [phase_gram(): lower = jnp.concatenate([phased_im, -phased_re], axis=-1)]
  transfers between devices with their start and end apart: 5 -> 4, of which waited for: 3 -> 3; matrix products, arithmetic and copies ran while one was open for 15% -> 2% of each run, Pallas kernels for 0% -> 6%
where the time goes in v1:
time: 145 us
  waiting for transfers between devices  78.6 us (54%)
  blocking collectives  20.1 us (14%)
  Pallas kernels  16.5 us (11%)
  between operations  13.2 us (9%)
  local copies, waits for them, and re-layouts  9.34 us (6%)
  matrix products  2.92 us (2%)
  other arithmetic  2.06 us (1%)
  starting transfers between devices  1.8 us (1%)
    all_gather x1, waiting for transfers between devices, local(): piece = lax.all_gather(tau, 'space', axis=1, tiled=True)  32.3 us
    reduce_scatter x1, waiting for transfers between devices, local(): lax.psum_scatter(sink_part, 'space', scatter_dimension=0, tiled=True)  27.5 us
    all_gather x1, blocking collectives, local(): source = lax.all_gather(share, 'space', axis=0, tiled=True)  20.1 us
    reduce_scatter x1, waiting for transfers between devices, local(): lax.psum_scatter(source_part, 'space', scatter_dimension=0, tiled=True)  18.6 us
    pallas_call x2, Pallas kernels, gram(): pl.pallas_call(functools.partial(gram_kernel, k), grid=(COLORS,), out_sha...  16.5 us
    unnamed x10, local copies, waits for them, and re-layouts  6.95 us
  transfers between devices with their start and end apart: 4, of which 3 were waited for; matrix products, arithmetic and copies ran while one was open for 2% of the time, Pallas kernels for 6%

profile of v1, /device:TPU:0, one launch (start us, length us, event | category | flops | bytes accessed | tf_op | source)
XLA Modules:
  0.0 144.5 jit_solution(8606638538423407828)
XLA Ops:
  6.5 0.0 reduce-scatter.5.cloned.1.call-start
  6.5 0.0 copy-start
  6.5 2.3 %copy-done = bf16[1,2,3,1024,384]{4,3,2,1,0:T(8,128)(2,1)S(1)} copy-done((bf16[1,2,3,1024,384]{4,3,2,1,0:T(8,128)(2,1)S(1)}, bf16[1,2,3,1024,384]{4,3,2,1,0:T(8,128)(2,1)}, u32[]{:S(2)}) %copy-start) | copy-done | bytes 4718616
  8.9 0.0 copy-start.2
  8.9 0.7 copy-done.2
  9.6 8.3 %shard_map.38 = f32[384,768]{1,0:T(8,128)} custom-call(s32[2,3]{1,0:T(2,128)S(1)} %copy-done.2, bf16[2,3,1024,384]{3,2,1,0:T(8,128)(2,1)S(1)} %bitcast.13), custom_call_target="tpu_custom_call" | custom-call | flops 3623878656 | bytes 4718592 | tf_op jit(solution)/shard_map/pallas_call | solution.py:83
  17.8 0.0 copy-start.3
  17.8 0.0 reduce-scatter.5.cloned.1.call-update
  17.9 0.0 reduce-scatter.3.cloned.1.call-start
  17.9 0.6 copy-done.3
  18.5 0.0 copy-start.1
  18.5 2.3 %copy-done.1 = bf16[1,2,3,1024,384]{4,3,2,1,0:T(8,128)(2,1)S(1)} copy-done((bf16[1,2,3,1024,384]{4,3,2,1,0:T(8,128)(2,1)S(1)}, bf16[1,2,3,1024,384]{4,3,2,1,0:T(8,128)(2,1)}, u32[]{:S(2)}) %copy-start.1) | copy-done | bytes 4718616
  20.8 8.3 %shard_map.37 = f32[384,768]{1,0:T(8,128)} custom-call(s32[2,3]{1,0:T(2,128)S(1)} %copy-done.3, bf16[2,3,1024,384]{3,2,1,0:T(8,128)(2,1)S(1)} %bitcast.14), custom_call_target="tpu_custom_call" | custom-call | flops 3623878656 | bytes 4718592 | tf_op jit(solution)/shard_map/pallas_call | solution.py:83
  29.1 0.0 copy-start.4
  29.1 0.0 reduce-scatter.3.cloned.1.call-update
  29.1 0.0 all-gather.2.cloned.1.call-start
  29.2 1.0 copy-done.4
  30.2 1.0 reshape_squeeze.9
  31.2 0.0 all-gather.2.cloned.1.call-update
  31.2 18.6 %reduce-scatter.5.cloned.1.call-done = f32[96,768]{1,0:T(8,128)} async-done(((f32[384,768]{1,0:T(8,128)}), f32[96,768]{1,0:T(8,128)}) %reduce-scatter.5.cloned.1.call-update) | async-done | bytes 294928 | tf_op jit(solution)/shard_map/reduce_scatter | solution.py:126
  49.9 1.0 convert_element_type.25
  50.9 1.7 %collective-permute-start = (bf16[96,768]{1,0:T(8,128)(2,1)S(1)}, bf16[96,768]{1,0:T(8,128)(2,1)S(1)}, u32[]{:S(2)}, u32[]{:S(2)}) collective-permute-start(bf16[96,768]{1,0:T(8,128)(2,1)S(1)} %convert_element_type.25), channel_id=1, source_target_pairs={{0,28},{4,24},{8,20},{12,16},{16,12},{20,8},{24,4},{28,0},{1,29},{... | collective-permute-start | bytes 442376 | tf_op jit(solution)/shard_map/ppermute | solution.py:131
  52.6 27.5 %reduce-scatter.3.cloned.1.call-done = f32[96,768]{1,0:T(8,128)} async-done(((f32[384,768]{1,0:T(8,128)}), f32[96,768]{1,0:T(8,128)}) %reduce-scatter.3.cloned.1.call-update) | async-done | bytes 294928 | tf_op jit(solution)/shard_map/reduce_scatter | solution.py:133
  80.1 1.0 convert_element_type.23
  81.2 0.0 collective-permute-done
  81.2 20.1 %all_gather.7 = bf16[384,768]{1,0:T(8,128)(2,1)S(1)} all-gather(bf16[96,768]{1,0:T(8,128)(2,1)S(1)} %collective-permute-done), channel_id=1, replica_groups=mesh['tm'=8,'space'=4] {'space'}, dimensions={0}, use_global_device_ids=true | all-gather | bytes 737280 | tf_op jit(solution)/shard_map/all_gather | solution.py:132
  101.3 0.1 slice_negate_fusion
  101.4 32.3 %all-gather.2.cloned.1.call-done = bf16[2,384,1536]{2,1,0:T(8,128)(2,1)} async-done(((bf16[2,96,1536]{2,1,0:T(8,128)(2,1)}), bf16[2,384,1536]{2,1,0:T(8,128)(2,1)}) %all-gather.2.cloned.1.call-update) | async-done | bytes 2359312 | tf_op jit(solution)/shard_map/all_gather | solution.py:136
  133.7 2.3 %convolution_convert_fusion = bf16[96,2,1536]{2,0,1:T(8,128)(2,1)S(1)} fusion(bf16[768,1536,1]{1,0,2:T(8,128)(2,1)} %bitcast.15, bf16[96,1,768]{2,0,1:T(8,128)(2,1)S(1)} %get-tuple-element.13, bf16[96,1,768]{2,0,1:T(8,128)(2,1)S(1)} %get-tuple-element.12), kind=kOutput, calls=%fused_computation | convolution fusion | flops 453427200 | bytes 3244032 | tf_op jit(solution)/shard_map/dot_general | solution.py:139
  136.0 0.2 reshape_squeeze.10
  136.2 0.2 reshape_squeeze.11
  136.4 0.6 convolution_convert_fusion.1
  137.1 0.9 convert_element_type.27
  (3 shorter events, 0.1 us)
Async XLA Ops:
  6.5 43.3 %reduce-scatter.5.cloned.1.call-start = ((), (), s32[]{:S(2)}) async-start(), calls=%async_computation.4 | async-start | bytes 1474560 | tf_op jit(solution)/shard_map/reduce_scatter | solution.py:126
  6.5 2.3 %copy-start = (bf16[1,2,3,1024,384]{4,3,2,1,0:T(8,128)(2,1)S(1)}, bf16[1,2,3,1024,384]{4,3,2,1,0:T(8,128)(2,1)}, u32[]{:S(2)}) copy-start(bf16[1,2,3,1024,384]{4,3,2,1,0:T(8,128)(2,1)} %param.3) | copy-start | bytes 14155780
  8.9 0.7 copy-start.2
  17.8 0.7 copy-start.3
  17.9 62.3 %reduce-scatter.3.cloned.1.call-start = ((), (), s32[]{:S(2)}) async-start(), calls=%async_computation.2 | async-start | bytes 1474560 | tf_op jit(solution)/shard_map/reduce_scatter | solution.py:133
  18.5 2.3 %copy-start.1 = (bf16[1,2,3,1024,384]{4,3,2,1,0:T(8,128)(2,1)S(1)}, bf16[1,2,3,1024,384]{4,3,2,1,0:T(8,128)(2,1)}, u32[]{:S(2)}) copy-start(bf16[1,2,3,1024,384]{4,3,2,1,0:T(8,128)(2,1)} %param.3) | copy-start | bytes 14155780
  29.1 1.1 copy-start.4
  29.1 104.6 %all-gather.2.cloned.1.call-start = ((), (), s32[]{:S(2)}) async-start(), calls=%async_computation.3 | async-start | bytes 2949120 | tf_op jit(solution)/shard_map/all_gather | solution.py:136
  50.9 30.3 %collective-permute-start = (bf16[96,768]{1,0:T(8,128)(2,1)S(1)}, bf16[96,768]{1,0:T(8,128)(2,1)S(1)}, u32[]{:S(2)}, u32[]{:S(2)}) collective-permute-start(bf16[96,768]{1,0:T(8,128)(2,1)S(1)} %convert_element_type.25), channel_id=1, source_target_pairs={{0,28},{4,24},{8,20},{12,16},{16,12},{20,8},{24,4},{28,0},{1,29},{... | collective-permute-start | bytes 442376 | tf_op jit(solution)/shard_map/ppermute | solution.py:131
Sparse Core Ops, SparseCore 0:
  18.0 31.8 reduce-scatter.4
  52.2 27.8 reduce-scatter.2
  81.7 51.9 all-gather.1

commit v2 on v1

v2 whole, which is shorter than its diff:
```python
import functools
import math

import jax
import jax.numpy as jnp
from jax import lax
from jax.experimental import pallas as pl
from jax.experimental.pallas import tpu as pltpu
from jax.sharding import PartitionSpec as P

SPIN = 4
COLORS = 3
LAT = 32
MESH = pl.DeviceIdType.MESH


def phase_tables(momenta_ref, k, first_site, count):
    sites = first_site + lax.broadcasted_iota(jnp.int32, (count, 128), 0)
    x = sites & (LAT - 1)
    y = (sites >> 5) & (LAT - 1)
    z = sites >> 10
    winding = (momenta_ref[k, 0] * x + momenta_ref[k, 1] * y + momenta_ref[k, 2] * z) & (LAT - 1)
    quadrant = (winding + 4) >> 3
    rest = (winding - (quadrant << 3)).astype(jnp.float32) * (2.0 * math.pi / LAT)
    sq = rest * rest
    sin_r = rest * (
        1.0 + sq * (-1.0 / 6 + sq * (1.0 / 120 + sq * (-1.0 / 5040 + sq * (1.0 / 362880))))
    )
    cos_r = 1.0 + sq * (
        -0.5 + sq * (1.0 / 24 + sq * (-1.0 / 720 + sq * (1.0 / 40320 + sq * (-1.0 / 3628800))))
    )
    odd = (quadrant & 1) == 1
    cos_q = jnp.where(odd, sin_r, cos_r)
    sin_q = jnp.where(odd, cos_r, sin_r)
    cos_t = jnp.where(((quadrant + 1) & 2) == 2, -cos_q, cos_q)
    sin_t = jnp.where((quadrant & 2) == 2, -sin_q, sin_q)
    return cos_t, sin_t


def fused_kernel(
    n,
    times,
    momenta_ref,
    vec_hbm,
    tau_ref,
    piece_ref,
    source_ref,
    block_ref,
    vec_ref,
    cos_ref,
    sin_ref,
    right_ref,
    acc_ref,
    part_ref,
    slots_ref,
    share_ref,
    load_sem,
    own_sem,
    hop_send,
    hop_recv,
    sum_send,
    sum_recv,
    all_send,
    all_recv,
):
    me_t = lax.axis_index("tm")
    me = lax.axis_index("space")
    other_t = times - 1 - me_t
    sites = vec_ref.shape[2]
    nvec = vec_ref.shape[3]
    nrows = share_ref.shape[0]

    def load(c):
        return pltpu.make_async_copy(vec_hbm.at[:, c], vec_ref.at[c], load_sem.at[c])

    for c in range(COLORS):
        load(c).start()
    own = pltpu.make_async_copy(tau_ref, piece_ref.at[me], own_sem)
    own.start()

    barrier = pltpu.get_barrier_semaphore()
    for d in range(n):
        peer = lax.rem(me + d, n)
        if d > 0:
            pl.semaphore_signal(barrier, 1, device_id=(me_t, peer), device_id_type=MESH)
        pl.semaphore_signal(barrier, 1, device_id=(other_t, peer), device_id_type=MESH)
    pl.semaphore_wait(barrier, 2 * n - 1)

    def hop(side, h, block, target):
        return pltpu.make_async_remote_copy(
            src_ref=tau_ref if h == 0 else piece_ref.at[block],
            dst_ref=piece_ref.at[block],
            send_sem=hop_send.at[side, h],
            recv_sem=hop_recv.at[side, h],
            device_id=(me_t, target),
            device_id_type=MESH,
        )

    def hop_out(side, h):
        if side == 0:
            return (me >= h) & (me + 1 < n), me - h, me + 1
        return (me + h < n) & (me >= 1), me + h, me - 1

    def hop_in(side, h):
        if side == 0:
            return me >= h + 1, me - 1 - h, me - 1
        return me + 1 + h < n, me + 1 + h, me + 1

    def start_hop(h):
        for side in range(2):
            active, block, target = hop_out(side, h)

            @pl.when(active)
            def _():
                hop(side, h, block, target).start()

    def finish_hop(h):
        for side in range(2):
            active, block, target = hop_in(side, h)

            @pl.when(active)
            def _():
                hop(side, h, block, target).wait_recv()

    def drain_hop(h):
        for side in range(2):
            active, block, target = hop_out(side, h)

            @pl.when(active)
            def _():
                hop(side, h, block, target).wait_send()

    start_hop(0)

    def tables(k):
        cos_t, sin_t = phase_tables(momenta_ref, k, me * sites, sites)
        cos_ref[...] = cos_t
        sin_ref[...] = sin_t

    def add_color(c):
        for lane in range(0, nvec, 128):
            real = vec_ref[c, 0, :, lane : lane + 128].astype(jnp.float32)
            imag = vec_ref[c, 1, :, lane : lane + 128].astype(jnp.float32)
            ph_re = (cos_ref[...] * real + sin_ref[...] * imag).astype(jnp.bfloat16)
            ph_im = (cos_ref[...] * imag - sin_ref[...] * real).astype(jnp.bfloat16)
            right_ref[:sites, lane : lane + 128] = ph_re
            right_ref[:sites, nvec + lane : nvec + lane + 128] = ph_im
            right_ref[sites:, lane : lane + 128] = ph_im
            right_ref[sites:, nvec + lane : nvec + lane + 128] = -ph_re
        acc_ref[...] += lax.dot_general(
            vec_ref[c].reshape(2 * sites, nvec),
            right_ref[...],
            (((0,), (0,)), ((), ())),
            preferred_element_type=jnp.float32,
        )

    def sum_copy(k, d):
        peer = lax.rem(me + d, n)
        return pltpu.make_async_remote_copy(
            src_ref=part_ref.at[k, peer],
            dst_ref=slots_ref.at[k, d - 1],
            send_sem=sum_send.at[k, d - 1],
            recv_sem=sum_recv.at[k, d - 1],
            device_id=(me_t, peer),
            device_id_type=MESH,
        )

    def send_parts(k):
        for j in range(n):
            part_ref[k, j] = acc_ref[j * nrows : (j + 1) * nrows, :].astype(jnp.bfloat16)
        for d in range(1, n):
            sum_copy(k, d).start()

    def summed(k):
        total = part_ref[k, me].astype(jnp.float32)
        for d in range(1, n):
            sum_copy(k, d).wait_recv()
            total = total + slots_ref[k, d - 1].astype(jnp.float32)
        return total.astype(jnp.bfloat16)

    tables(1)
    acc_ref[...] = jnp.zeros_like(acc_ref)

    def source_color(c, carry):
        load(c).wait()
        add_color(c)
        return carry

    lax.fori_loop(0, COLORS, source_color, 0)
    send_parts(1)

    tables(0)
    acc_ref[...] = jnp.zeros_like(acc_ref)

    def sink_color(c, carry):
        add_color(c)
        return carry

    lax.fori_loop(0, COLORS, sink_color, 0)
    send_parts(0)

    share_ref[...] = summed(1)

    def spread(d):
        peer = lax.rem(me + d, n)
        return pltpu.make_async_remote_copy(
            src_ref=share_ref,
            dst_ref=source_ref.at[me],
            send_sem=all_send.at[d],
            recv_sem=all_recv.at[me],
            device_id=(other_t, peer),
            device_id_type=MESH,
        )

    def arrival(j):
        return pltpu.make_async_remote_copy(
            src_ref=share_ref,
            dst_ref=source_ref.at[j],
            send_sem=all_send.at[j],
            recv_sem=all_recv.at[j],
            device_id=(other_t, j),
            device_id_type=MESH,
        )

    for d in range(n):
        spread(d).start()
    for h in range(n - 1):
        finish_hop(h)
        if h + 1 < n - 1:
            start_hop(h + 1)
        if h == 0:
            block_ref[...] = summed(0)
    own.wait()
    for j in range(n):
        arrival(j).wait_recv()
    for d in range(n):
        spread(d).wait_send()
        if d > 0:
            sum_copy(1, d).wait_send()
            sum_copy(0, d).wait_send()
    for h in range(n - 1):
        drain_hop(h)


def fused(vectors, momenta, tau):
    n = lax.axis_size("space")
    times = lax.axis_size("tm")
    sites = vectors.shape[2]
    nvec = vectors.shape[3]
    nrows = tau.shape[1]
    width = tau.shape[2]
    kind = jnp.bfloat16
    return pl.pallas_call(
        functools.partial(fused_kernel, n, times),
        out_shape=(
            jax.ShapeDtypeStruct((n, 2, nrows, width), kind),
            jax.ShapeDtypeStruct((n, nrows, 2 * nvec), kind),
            jax.ShapeDtypeStruct((nrows, 2 * nvec), kind),
        ),
        in_specs=[
            pl.BlockSpec(memory_space=pltpu.SMEM),
            pl.BlockSpec(memory_space=pl.ANY),
            pl.BlockSpec(memory_space=pl.ANY),
        ],
        out_specs=(
            pl.BlockSpec(memory_space=pl.ANY),
            pl.BlockSpec(memory_space=pl.ANY),
            pl.BlockSpec(memory_space=pltpu.VMEM),
        ),
        scratch_shapes=[
            pltpu.VMEM((COLORS, 2, sites, nvec), kind),
            pltpu.VMEM((sites, 128), jnp.float32),
            pltpu.VMEM((sites, 128), jnp.float32),
            pltpu.VMEM((2 * sites, 2 * nvec), kind),
            pltpu.VMEM((nvec, 2 * nvec), jnp.float32),
            pltpu.VMEM((2, n, nrows, 2 * nvec), kind),
            pltpu.VMEM((2, n - 1, nrows, 2 * nvec), kind),
            pltpu.VMEM((nrows, 2 * nvec), kind),
            pltpu.SemaphoreType.DMA((COLORS,)),
            pltpu.SemaphoreType.DMA,
            pltpu.SemaphoreType.DMA((2, n - 1)),
            pltpu.SemaphoreType.DMA((2, n - 1)),
            pltpu.SemaphoreType.DMA((2, n - 1)),
            pltpu.SemaphoreType.DMA((2, n - 1)),
            pltpu.SemaphoreType.DMA((n,)),
            pltpu.SemaphoreType.DMA((n,)),
        ],
        compiler_params=pltpu.CompilerParams(
            collective_id=0, has_side_effects=True, vmem_limit_bytes=44 * 1024 * 1024
        ),
        cost_estimate=pl.CostEstimate(
            flops=16 * COLORS * sites * nvec * nvec,
            bytes_accessed=4 * COLORS * sites * nvec,
            transcendentals=0,
        ),
    )(momenta, vectors, tau)


def complex_left(block_re, block_im, n):
    rows = block_re.shape[0]
    cols = block_re.shape[1]
    block_re = block_re.reshape(rows, n, cols // n)
    block_im = block_im.reshape(rows, n, cols // n)
    stacked = jnp.stack(
        [jnp.stack([block_re, -block_im], axis=2), jnp.stack([block_im, block_re], axis=2)], axis=1
    )
    return stacked.reshape(2 * rows, 2 * cols)


def local(eigvec, momenta, peram):
    vectors = eigvec[0]
    nvec = vectors.shape[3]
    nrows = peram.shape[2]
    tau = peram[0].reshape(2, nrows, SPIN * nvec)
    piece, source, block = fused(vectors, momenta, tau)
    n = piece.shape[0]
    source = source.reshape(nvec, 2 * nvec)
    flat = piece.reshape(2 * nvec, SPIN * nvec)
    mixed = jnp.dot(
        complex_left(block[:, :nvec], block[:, nvec:], n), flat, preferred_element_type=jnp.float32
    ).reshape(nrows, 2, SPIN * nvec)
    mixed = mixed.astype(jnp.bfloat16)
    mixed_re = mixed[:, 0].reshape(nrows * SPIN, nvec)
    mixed_im = mixed[:, 1].reshape(nrows * SPIN, nvec)
    source_re = source[:, :nvec]
    source_im = source[:, nvec:]
    right = jnp.concatenate([source, jnp.concatenate([-source_im, source_re], axis=1)], axis=0)
    dressed = jnp.dot(
        jnp.concatenate([mixed_re, mixed_im], axis=1), right, preferred_element_type=jnp.float32
    )
    return dressed.reshape(1, nrows, SPIN, 2, nvec).astype(jnp.bfloat16)


def solution(mesh):
    return jax.shard_map(
        local,
        mesh=mesh,
        in_specs=(P("tm", None, None, "space", None), P(), P("tm", None, "space", None, None)),
        out_specs=P("tm", "space", None, None, None),
        check_vma=False,
    )
```

time: 145 us -> 95.3 us (0.66)
  waiting for transfers between devices: 78.6 us -> 0 us
  Pallas kernels: 16.5 us -> 87.4 us
  blocking collectives: 20.1 us -> 0 us
  between operations: 13.2 us -> 0.12 us
  local copies, waits for them, and re-layouts: 9.34 us -> 6.14 us
  other arithmetic: 2.06 us -> 0.16 us
  starting transfers between devices: 1.8 us -> 0 us
  matrix products: 2.92 us -> 1.33 us
    pallas_call x2 -> x1, Pallas kernels: 16.5 us -> 87.4 us  [fused(): pl.pallas_call(functools.partial(fused_kernel, n, times), out_shape=(jax....]
    reduce_scatter x2 -> x0, waiting for transfers between devices: 46.2 us -> none  [the longest x1 27.5 us: local(): lax.psum_scatter(sink_part, 'space', scatter_dimension=0, tiled=True)]
    all_gather x1 -> x0, waiting for transfers between devices: 32.3 us -> none  [local(): piece = lax.all_gather(tau, 'space', axis=1, tiled=True)]
    all_gather x1 -> x0, blocking collectives: 20.1 us -> none  [local(): source = lax.all_gather(share, 'space', axis=0, tiled=True)]
    unnamed x10 -> x4, local copies, waits for them, and re-layouts: 6.95 us -> 3.01 us
    convert_element_type x2 -> x0, other arithmetic: 1.96 us -> none  [the longest x1 0.98 us: local(): lax.psum_scatter(source_part, 'space', scatter_dimension=0, tiled=True)]
    ppermute x1 -> x0, starting transfers between devices: 1.72 us -> none  [local(): lax.ppermute(share, 'tm', [(i, times - 1 - i) for i in range(times)])]
    dot_general x1, matrix products: 2.29 us -> 0.69 us  [local(): jnp.dot(complex_left(block[:, :nvec], block[:, nvec:], n), flat, preferre...]
  transfers between devices with their start and end apart: 4 -> 0, of which waited for: 3 -> 0; matrix products, arithmetic and copies ran while one was open for 2% -> 0% of each run, Pallas kernels for 6% -> 0%
where the time goes in v2:
time: 95.3 us; the launch traced here: 95.1 us
  Pallas kernels  87.4 us (92%)
  local copies, waits for them, and re-layouts  6.14 us (6%)
  matrix products  1.33 us (1%)
    pallas_call x1, Pallas kernels, fused(): pl.pallas_call(functools.partial(fused_kernel, n, times), out_shape=(jax....  87.4 us
    unnamed x4, local copies, waits for them, and re-layouts  3.01 us

profile of v2, /device:TPU:0, one launch (start us, length us, event | category | flops | bytes accessed | tf_op | source)
XLA Modules:
  0.0 95.1 jit_solution(2297724591588888021)
XLA Ops:
  0.0 1.5 %reshape_squeeze.9.tau_ref = bf16[2,96,1536]{2,1,0:T(8,128)(2,1)S(1)} reshape(bf16[1,2,96,4,384]{4,3,2,1,0:T(4,128)(2,1)} %param.5) | data formatting | bytes 1179648 | tf_op jit(solution)/shard_map/reshape;squeeze | solution.py:314
  1.5 0.0 copy-start
  1.5 2.3 %copy-done = bf16[1,2,3,1024,384]{4,3,2,1,0:T(8,128)(2,1)S(1)} copy-done((bf16[1,2,3,1024,384]{4,3,2,1,0:T(8,128)(2,1)S(1)}, bf16[1,2,3,1024,384]{4,3,2,1,0:T(8,128)(2,1)}, u32[]{:S(2)}) %copy-start) | copy-done | bytes 4718616
  3.9 0.0 copy-start.1
  3.9 0.7 copy-done.1
  4.5 87.4 %shard_map.37 = (bf16[4,2,96,1536]{3,2,1,0:T(8,128)(2,1)S(1)}, bf16[4,96,768]{2,1,0:T(8,128)(2,1)S(1)}, bf16[96,768]{1,0:T(8,128)(2,1)S(1)}) custom-call(s32[2,3]{1,0:T(2,128)S(1)} %copy-done.1, bf16[2,3,1024,384]{3,2,1,0:T(8,128)(2,1)S(1)} %bitcast.27, bf16[2,96,1536]{2,1,0:T(8,128)(2,1)S(1)} %reshape_squeeze.9.tau_ref), custom_call_target="tpu_custom_call" | custom-call | flops 7247757312 | bytes 4718592 | tf_op jit(solution)/shard_map/pallas_call | solution.py:253
  92.0 0.1 reshape.35
  92.1 0.1 stack_reshape.2
  92.2 0.1 maximum_bitcast_fusion
  92.3 0.7 fusion
  93.1 0.2 reshape_squeeze.10
  93.3 0.2 reshape_squeeze.11
  93.5 0.1 slice_negate_fusion
  93.5 0.6 convolution_convert_fusion
  94.2 0.9 convert_element_type.19
  (4 shorter events, 0.1 us)
Async XLA Ops:
  1.5 2.3 %copy-start = (bf16[1,2,3,1024,384]{4,3,2,1,0:T(8,128)(2,1)S(1)}, bf16[1,2,3,1024,384]{4,3,2,1,0:T(8,128)(2,1)}, u32[]{:S(2)}) copy-start(bf16[1,2,3,1024,384]{4,3,2,1,0:T(8,128)(2,1)} %param.3) | copy-start | bytes 14155780
  3.9 0.7 copy-start.1

commit v3 on v2

--- a/solution.py
+++ b/solution.py
@@ -51,8 +51,9 @@
     sin_ref,
     right_ref,
     acc_ref,
-    part_ref,
-    slots_ref,
+    inbox_ref,
+    outbox_ref,
+    total_ref,
     share_ref,
     load_sem,
     own_sem,
@@ -137,7 +138,7 @@
         cos_ref[...] = cos_t
         sin_ref[...] = sin_t
 
-    def add_color(c):
+    def add_color(k, c):
         for lane in range(0, nvec, 128):
             real = vec_ref[c, 0, :, lane : lane + 128].astype(jnp.float32)
             imag = vec_ref[c, 1, :, lane : lane + 128].astype(jnp.float32)
@@ -147,57 +148,105 @@
             right_ref[:sites, nvec + lane : nvec + lane + 128] = ph_im
             right_ref[sites:, lane : lane + 128] = ph_im
             right_ref[sites:, nvec + lane : nvec + lane + 128] = -ph_re
-        acc_ref[...] += lax.dot_general(
+        acc_ref[k] += lax.dot_general(
             vec_ref[c].reshape(2 * sites, nvec),
             right_ref[...],
             (((0,), (0,)), ((), ())),
             preferred_element_type=jnp.float32,
         )
 
-    def sum_copy(k, d):
-        peer = lax.rem(me + d, n)
+    def sum_copy(k, side, j):
         return pltpu.make_async_remote_copy(
-            src_ref=part_ref.at[k, peer],
-            dst_ref=slots_ref.at[k, d - 1],
-            send_sem=sum_send.at[k, d - 1],
-            recv_sem=sum_recv.at[k, d - 1],
-            device_id=(me_t, peer),
+            src_ref=outbox_ref.at[k, side, j],
+            dst_ref=inbox_ref.at[k, side, j],
+            send_sem=sum_send.at[k, side, j],
+            recv_sem=sum_recv.at[k, side, j],
+            device_id=(me_t, me + 1 if side == 0 else me - 1),
             device_id_type=MESH,
         )
 
-    def send_parts(k):
-        for j in range(n):
-            part_ref[k, j] = acc_ref[j * nrows : (j + 1) * nrows, :].astype(jnp.bfloat16)
-        for d in range(1, n):
-            sum_copy(k, d).start()
+    def rows_of(k, j):
+        return acc_ref[k, j * nrows : (j + 1) * nrows, :]
+
+    legs = []
+    for i in range(1, n):
+        legs.append((0, n - i))
+        legs.append((1, i - 1))
+
+    def leg_state(side, j):
+        if side == 0:
+            return me < j, me == 0
+        return me > j, me == n - 1
+
+    def begin_sums(k):
+        for side, j in legs:
+            active, first = leg_state(side, j)
+
+            @pl.when(active & first)
+            def _():
+                outbox_ref[k, side, j] = rows_of(k, j).astype(jnp.bfloat16)
+                sum_copy(k, side, j).start()
+
+    def pass_sums(k):
+        for side, j in legs:
+            active, first = leg_state(side, j)
+
+            @pl.when(active & jnp.logical_not(first))
+            def _():
+                sum_copy(k, side, j).wait_recv()
+                outbox_ref[k, side, j] = (
+                    rows_of(k, j) + inbox_ref[k, side, j].astype(jnp.float32)
+                ).astype(jnp.bfloat16)
+                sum_copy(k, side, j).start()
 
     def summed(k):
-        total = part_ref[k, me].astype(jnp.float32)
-        for d in range(1, n):
-            sum_copy(k, d).wait_recv()
-            total = total + slots_ref[k, d - 1].astype(jnp.float32)
-        return total.astype(jnp.bfloat16)
+        total_ref[...] = acc_ref[k, pl.ds(pl.multiple_of(me * nrows, 8), nrows), :]
+
+        @pl.when(me > 0)
+        def _():
+            sum_copy(k, 0, me).wait_recv()
+            total_ref[...] += inbox_ref[k, 0, me].astype(jnp.float32)
+
+        @pl.when(me < n - 1)
+        def _():
+            sum_copy(k, 1, me).wait_recv()
+            total_ref[...] += inbox_ref[k, 1, me].astype(jnp.float32)
+
+        return total_ref[...].astype(jnp.bfloat16)
+
+    def drain_sums(k):
+        for side, j in legs:
+            active, first = leg_state(side, j)
+
+            @pl.when(active)
+            def _():
+                sum_copy(k, side, j).wait_send()
+
+    acc_ref[...] = jnp.zeros_like(acc_ref)
 
     tables(1)
-    acc_ref[...] = jnp.zeros_like(acc_ref)
 
     def source_color(c, carry):
         load(c).wait()
-        add_color(c)
+        add_color(1, c)
         return carry
 
     lax.fori_loop(0, COLORS, source_color, 0)
-    send_parts(1)
+    begin_sums(1)
 
     tables(0)
-    acc_ref[...] = jnp.zeros_like(acc_ref)
 
     def sink_color(c, carry):
-        add_color(c)
+        add_color(0, c)
         return carry
 
-    lax.fori_loop(0, COLORS, sink_color, 0)
-    send_parts(0)
+    lax.fori_loop(0, COLORS - 1, sink_color, 0)
+    finish_hop(0)
+    if n > 2:
+        start_hop(1)
+    lax.fori_loop(COLORS - 1, COLORS, sink_color, 0)
+    begin_sums(0)
+    pass_sums(1)
 
     share_ref[...] = summed(1)
 
@@ -224,20 +273,19 @@
 
     for d in range(n):
         spread(d).start()
-    for h in range(n - 1):
+    pass_sums(0)
+    block_ref[...] = summed(0)
+    for h in range(1, n - 1):
         finish_hop(h)
         if h + 1 < n - 1:
             start_hop(h + 1)
-        if h == 0:
-            block_ref[...] = summed(0)
     own.wait()
     for j in range(n):
         arrival(j).wait_recv()
     for d in range(n):
         spread(d).wait_send()
-        if d > 0:
-            sum_copy(1, d).wait_send()
-            sum_copy(0, d).wait_send()
+    drain_sums(1)
+    drain_sums(0)
     for h in range(n - 1):
         drain_hop(h)
 
@@ -272,21 +320,22 @@
             pltpu.VMEM((sites, 128), jnp.float32),
             pltpu.VMEM((sites, 128), jnp.float32),
             pltpu.VMEM((2 * sites, 2 * nvec), kind),
-            pltpu.VMEM((nvec, 2 * nvec), jnp.float32),
-            pltpu.VMEM((2, n, nrows, 2 * nvec), kind),
-            pltpu.VMEM((2, n - 1, nrows, 2 * nvec), kind),
+            pltpu.VMEM((2, nvec, 2 * nvec), jnp.float32),
+            pltpu.VMEM((2, 2, n, nrows, 2 * nvec), kind),
+            pltpu.VMEM((2, 2, n, nrows, 2 * nvec), kind),
+            pltpu.VMEM((nrows, 2 * nvec), jnp.float32),
             pltpu.VMEM((nrows, 2 * nvec), kind),
             pltpu.SemaphoreType.DMA((COLORS,)),
             pltpu.SemaphoreType.DMA,
             pltpu.SemaphoreType.DMA((2, n - 1)),
             pltpu.SemaphoreType.DMA((2, n - 1)),
-            pltpu.SemaphoreType.DMA((2, n - 1)),
-            pltpu.SemaphoreType.DMA((2, n - 1)),
+            pltpu.SemaphoreType.DMA((2, 2, n)),
+            pltpu.SemaphoreType.DMA((2, 2, n)),
             pltpu.SemaphoreType.DMA((n,)),
             pltpu.SemaphoreType.DMA((n,)),
         ],
         compiler_params=pltpu.CompilerParams(
-            collective_id=0, has_side_effects=True, vmem_limit_bytes=44 * 1024 * 1024
+            collective_id=0, has_side_effects=True, vmem_limit_bytes=60 * 1024 * 1024
         ),
         cost_estimate=pl.CostEstimate(
             flops=16 * COLORS * sites * nvec * nvec,

time: 95.3 us -> 103 us (1.081)
  Pallas kernels: 87.4 us -> 95 us
  matrix products: 1.33 us -> 3.04 us
  local copies, waits for them, and re-layouts: 6.14 us -> 4.77 us
    pallas_call x1, Pallas kernels: 87.4 us -> 95 us  [fused(): pl.pallas_call(functools.partial(fused_kernel, n, times), out_shape=(jax....]
    unnamed x4 -> x2, local copies, waits for them, and re-layouts: 3.01 us -> 0.01 us
    dot_general x1, matrix products: 0.69 us -> 2.41 us  [local(): jnp.dot(complex_left(block[:, :nvec], block[:, nvec:], n), flat, preferre...]
where the time goes in v3:
time: 103 us
  Pallas kernels  95 us (92%)
  local copies, waits for them, and re-layouts  4.77 us (5%)
  matrix products  3.04 us (3%)
    pallas_call x1, Pallas kernels, fused(): pl.pallas_call(functools.partial(fused_kernel, n, times), out_shape=(jax....  95 us
    dot_general x1, matrix products, local(): jnp.dot(complex_left(block[:, :nvec], block[:, nvec:], n), flat, preferre...  2.41 us
    another operation x1, local copies, waits for them, and re-layouts, local(): tau = peram[0].reshape(2, nrows, SPIN * nvec)  2.24 us

profile of v3, /device:TPU:0, one launch (start us, length us, event | category | flops | bytes accessed | tf_op | source)
XLA Modules:
  0.0 103.0 jit_solution(2806369566470137689)
XLA Ops:
  0.0 2.2 %reshape_squeeze.9.tau_ref = bf16[2,96,1536]{2,1,0:T(8,128)(2,1)} reshape(bf16[1,2,96,4,384]{4,3,2,1,0:T(4,128)(2,1)} %param.5) | data formatting | bytes 1179648 | tf_op jit(solution)/shard_map/reshape;squeeze | solution.py:363
  2.2 95.0 %shard_map.37 = (bf16[4,2,96,1536]{3,2,1,0:T(8,128)(2,1)}, bf16[4,96,768]{2,1,0:T(8,128)(2,1)}, bf16[96,768]{1,0:T(8,128)(2,1)}) custom-call(s32[2,3]{1,0:T(2,128)} %momenta_ref.1, bf16[2,3,1024,384]{3,2,1,0:T(8,128)(2,1)} %bitcast.27, bf16[2,96,1536]{2,1,0:T(8,128)(2,1)} %reshape_squeeze.9.tau_ref), custom_call_target="tpu_custom_call" | custom-call | flops 7247757312 | bytes 4718592 | tf_op jit(solution)/shard_map/pallas_call | solution.py:301
  97.2 0.9 fusion.16
  98.2 0.1 reshape.35
  98.3 0.1 stack_reshape.2
  98.4 0.1 maximum_bitcast_fusion
  98.5 0.0 copy-start
  98.5 2.4 %fusion = bf16[96,2,1536]{2,0,1:T(8,128)(2,1)S(1)} fusion(bf16[4,2,96,1536]{3,2,1,0:T(8,128)(2,1)} %get-tuple-element.9, bf16[96,1,4,2,96]{4,0,3,2,1:T(8,128)(2,1)S(1)} %get-tuple-element.18, bf16[96,1,4,2,96]{4,0,3,2,1:T(8,128)(2,1)S(1)} %get-tuple-element.17), kind=kOutput, calls=%fused_computation.1 | convolution fusion | flops 453427200 | bytes 3244032 | tf_op jit(solution)/shard_map/dot_general | solution.py:368
  101.0 0.2 reshape_squeeze.10
  101.2 0.2 reshape_squeeze.11
  101.4 0.0 copy-done
  101.4 0.1 slice_negate_fusion
  101.5 0.6 convolution_convert_fusion
  102.1 0.9 convert_element_type.19
  (3 shorter events, 0.1 us)
Async XLA Ops:
  98.5 2.9 %copy-start = (bf16[4,96,768]{2,1,0:T(8,128)(2,1)S(1)}, bf16[4,96,768]{2,1,0:T(8,128)(2,1)}, u32[]{:S(2)}) copy-start(bf16[4,96,768]{2,1,0:T(8,128)(2,1)} %get-tuple-element.10) | copy-start | bytes 1769476

commit v4 on v2

--- a/solution.py
+++ b/solution.py
@@ -86,12 +86,12 @@
         pl.semaphore_signal(barrier, 1, device_id=(other_t, peer), device_id_type=MESH)
     pl.semaphore_wait(barrier, 2 * n - 1)
 
-    def hop(side, h, block, target):
+    def hop(side, h, part, block, target):
         return pltpu.make_async_remote_copy(
-            src_ref=tau_ref if h == 0 else piece_ref.at[block],
-            dst_ref=piece_ref.at[block],
-            send_sem=hop_send.at[side, h],
-            recv_sem=hop_recv.at[side, h],
+            src_ref=tau_ref.at[part] if h == 0 else piece_ref.at[block, part],
+            dst_ref=piece_ref.at[block, part],
+            send_sem=hop_send.at[side, h, part],
+            recv_sem=hop_recv.at[side, h, part],
             device_id=(me_t, target),
             device_id_type=MESH,
         )
@@ -106,21 +106,29 @@
             return me >= h + 1, me - 1 - h, me - 1
         return me + 1 + h < n, me + 1 + h, me + 1
 
-    def start_hop(h):
+    def start_hop(h, part):
         for side in range(2):
             active, block, target = hop_out(side, h)
 
             @pl.when(active)
             def _():
-                hop(side, h, block, target).start()
+                hop(side, h, part, block, target).start()
 
     def finish_hop(h):
-        for side in range(2):
-            active, block, target = hop_in(side, h)
-
-            @pl.when(active)
-            def _():
-                hop(side, h, block, target).wait_recv()
+        for part in range(2):
+            for side in range(2):
+                active, block, target = hop_in(side, h)
+
+                @pl.when(active)
+                def _():
+                    hop(side, h, part, block, target).wait_recv()
+
+                if h + 1 < n - 1:
+                    go, onward, after = hop_out(side, h + 1)
+
+                    @pl.when(go)
+                    def _():
+                        hop(side, h + 1, part, onward, after).start()
 
     def drain_hop(h):
         for side in range(2):
@@ -128,9 +136,11 @@
 
             @pl.when(active)
             def _():
-                hop(side, h, block, target).wait_send()
-
-    start_hop(0)
+                for part in range(2):
+                    hop(side, h, part, block, target).wait_send()
+
+    for part in range(2):
+        start_hop(0, part)
 
     def tables(k):
         cos_t, sin_t = phase_tables(momenta_ref, k, me * sites, sites)
@@ -196,7 +206,9 @@
         add_color(c)
         return carry
 
-    lax.fori_loop(0, COLORS, sink_color, 0)
+    lax.fori_loop(0, COLORS - 1, sink_color, 0)
+    finish_hop(0)
+    lax.fori_loop(COLORS - 1, COLORS, sink_color, 0)
     send_parts(0)
 
     share_ref[...] = summed(1)
@@ -224,12 +236,9 @@
 
     for d in range(n):
         spread(d).start()
-    for h in range(n - 1):
+    for h in range(1, n - 1):
         finish_hop(h)
-        if h + 1 < n - 1:
-            start_hop(h + 1)
-        if h == 0:
-            block_ref[...] = summed(0)
+    block_ref[...] = summed(0)
     own.wait()
     for j in range(n):
         arrival(j).wait_recv()
@@ -278,8 +287,8 @@
             pltpu.VMEM((nrows, 2 * nvec), kind),
             pltpu.SemaphoreType.DMA((COLORS,)),
             pltpu.SemaphoreType.DMA,
-            pltpu.SemaphoreType.DMA((2, n - 1)),
-            pltpu.SemaphoreType.DMA((2, n - 1)),
+            pltpu.SemaphoreType.DMA((2, n - 1, 2)),
+            pltpu.SemaphoreType.DMA((2, n - 1, 2)),
             pltpu.SemaphoreType.DMA((2, n - 1)),
             pltpu.SemaphoreType.DMA((2, n - 1)),
             pltpu.SemaphoreType.DMA((n,)),

time: 95.3 us -> 84.4 us (0.89)
  Pallas kernels: 87.4 us -> 76.4 us
    pallas_call x1, Pallas kernels: 87.4 us -> 76.4 us  [fused(): pl.pallas_call(functools.partial(fused_kernel, n, times), out_shape=(jax....]
where the time goes in v4:
time: 84.4 us; the launch traced here: 84.2 us
  Pallas kernels  76.4 us (91%)
  local copies, waits for them, and re-layouts  6.14 us (7%)
  matrix products  1.32 us (2%)
    pallas_call x1, Pallas kernels, fused(): pl.pallas_call(functools.partial(fused_kernel, n, times), out_shape=(jax....  76.4 us
    unnamed x4, local copies, waits for them, and re-layouts  3.01 us

profile of v4, /device:TPU:0, one launch (start us, length us, event | category | flops | bytes accessed | tf_op | source)
XLA Modules:
  0.0 84.2 jit_solution(10800846150205075856)
XLA Ops:
  0.0 1.5 %reshape_squeeze.9.tau_ref = bf16[2,96,1536]{2,1,0:T(8,128)(2,1)S(1)} reshape(bf16[1,2,96,4,384]{4,3,2,1,0:T(4,128)(2,1)} %param.5) | data formatting | bytes 1179648 | tf_op jit(solution)/shard_map/reshape;squeeze | solution.py:323
  1.5 0.0 copy-start
  1.5 2.3 %copy-done = bf16[1,2,3,1024,384]{4,3,2,1,0:T(8,128)(2,1)S(1)} copy-done((bf16[1,2,3,1024,384]{4,3,2,1,0:T(8,128)(2,1)S(1)}, bf16[1,2,3,1024,384]{4,3,2,1,0:T(8,128)(2,1)}, u32[]{:S(2)}) %copy-start) | copy-done | bytes 4718616
  3.9 0.0 copy-start.1
  3.9 0.7 copy-done.1
  4.5 76.4 %shard_map.37 = (bf16[4,2,96,1536]{3,2,1,0:T(8,128)(2,1)S(1)}, bf16[4,96,768]{2,1,0:T(8,128)(2,1)S(1)}, bf16[96,768]{1,0:T(8,128)(2,1)S(1)}) custom-call(s32[2,3]{1,0:T(2,128)S(1)} %copy-done.1, bf16[2,3,1024,384]{3,2,1,0:T(8,128)(2,1)S(1)} %bitcast.27, bf16[2,96,1536]{2,1,0:T(8,128)(2,1)S(1)} %reshape_squeeze.9.tau_ref), custom_call_target="tpu_custom_call" | custom-call | flops 7247757312 | bytes 4718592 | tf_op jit(solution)/shard_map/pallas_call | solution.py:262
  81.0 0.1 reshape.35
  81.1 0.1 stack_reshape.2
  81.3 0.1 maximum_bitcast_fusion
  81.4 0.7 fusion
  82.1 0.2 reshape_squeeze.10
  82.3 0.2 reshape_squeeze.11
  82.5 0.1 slice_negate_fusion
  82.6 0.6 convolution_convert_fusion
  83.2 0.9 %convert_element_type.19 = bf16[1,96,4,2,384]{4,3,2,1,0:T(2,128)(2,1)} reshape(bf16[384,768]{1,0:T(8,128)(2,1)S(1)} %convolution_convert_fusion) | data formatting | bytes 1179648 | tf_op jit(solution)/shard_map/convert_element_type | solution.py:340
  (4 shorter events, 0.1 us)
Async XLA Ops:
  1.5 2.3 %copy-start = (bf16[1,2,3,1024,384]{4,3,2,1,0:T(8,128)(2,1)S(1)}, bf16[1,2,3,1024,384]{4,3,2,1,0:T(8,128)(2,1)}, u32[]{:S(2)}) copy-start(bf16[1,2,3,1024,384]{4,3,2,1,0:T(8,128)(2,1)} %param.3) | copy-start | bytes 14155780
  3.9 0.7 copy-start.1

commit v5 on v4

--- a/solution.py
+++ b/solution.py
@@ -236,9 +236,11 @@
 
     for d in range(n):
         spread(d).start()
-    for h in range(1, n - 1):
+    for h in range(1, n - 2):
         finish_hop(h)
     block_ref[...] = summed(0)
+    if n > 2:
+        finish_hop(n - 2)
     own.wait()
     for j in range(n):
         arrival(j).wait_recv()

time: 84.4 us -> 84.2 us (level)
  no operation moved by 1% of the time
where the time goes in v5:
time: 84.2 us; the launch traced here: 84.1 us
  Pallas kernels  76.3 us (91%)
  local copies, waits for them, and re-layouts  6.14 us (7%)
  matrix products  1.32 us (2%)
    pallas_call x1, Pallas kernels, fused(): pl.pallas_call(functools.partial(fused_kernel, n, times), out_shape=(jax....  76.3 us
    unnamed x4, local copies, waits for them, and re-layouts  3.01 us

profile of v5, /device:TPU:0, one launch (start us, length us, event | category | flops | bytes accessed | tf_op | source)
XLA Modules:
  0.0 84.1 jit_solution(9183929046246274698)
XLA Ops:
  0.0 1.5 %reshape_squeeze.9.tau_ref = bf16[2,96,1536]{2,1,0:T(8,128)(2,1)S(1)} reshape(bf16[1,2,96,4,384]{4,3,2,1,0:T(4,128)(2,1)} %param.5) | data formatting | bytes 1179648 | tf_op jit(solution)/shard_map/reshape;squeeze | solution.py:325
  1.5 0.0 copy-start
  1.5 2.3 %copy-done = bf16[1,2,3,1024,384]{4,3,2,1,0:T(8,128)(2,1)S(1)} copy-done((bf16[1,2,3,1024,384]{4,3,2,1,0:T(8,128)(2,1)S(1)}, bf16[1,2,3,1024,384]{4,3,2,1,0:T(8,128)(2,1)}, u32[]{:S(2)}) %copy-start) | copy-done | bytes 4718616
  3.9 0.0 copy-start.1
  3.9 0.7 copy-done.1
  4.5 76.3 %shard_map.37 = (bf16[4,2,96,1536]{3,2,1,0:T(8,128)(2,1)S(1)}, bf16[4,96,768]{2,1,0:T(8,128)(2,1)S(1)}, bf16[96,768]{1,0:T(8,128)(2,1)S(1)}) custom-call(s32[2,3]{1,0:T(2,128)S(1)} %copy-done.1, bf16[2,3,1024,384]{3,2,1,0:T(8,128)(2,1)S(1)} %bitcast.27, bf16[2,96,1536]{2,1,0:T(8,128)(2,1)S(1)} %reshape_squeeze.9.tau_ref), custom_call_target="tpu_custom_call" | custom-call | flops 7247757312 | bytes 4718592 | tf_op jit(solution)/shard_map/pallas_call | solution.py:264
  80.9 0.1 reshape.35
  81.0 0.1 stack_reshape.2
  81.2 0.1 maximum_bitcast_fusion
  81.3 0.7 fusion
  82.0 0.2 reshape_squeeze.10
  82.2 0.2 reshape_squeeze.11
  82.4 0.1 slice_negate_fusion
  82.5 0.6 convolution_convert_fusion
  83.1 0.9 %convert_element_type.19 = bf16[1,96,4,2,384]{4,3,2,1,0:T(2,128)(2,1)} reshape(bf16[384,768]{1,0:T(8,128)(2,1)S(1)} %convolution_convert_fusion) | data formatting | bytes 1179648 | tf_op jit(solution)/shard_map/convert_element_type | solution.py:342
  (4 shorter events, 0.1 us)
Async XLA Ops:
  1.5 2.3 %copy-start = (bf16[1,2,3,1024,384]{4,3,2,1,0:T(8,128)(2,1)S(1)}, bf16[1,2,3,1024,384]{4,3,2,1,0:T(8,128)(2,1)}, u32[]{:S(2)}) copy-start(bf16[1,2,3,1024,384]{4,3,2,1,0:T(8,128)(2,1)} %param.3) | copy-start | bytes 14155780
  3.9 0.7 copy-start.1
